TPU v7x, 32 devices: a whole 2x2x4 slice. The times are simulated.
32 devices in a mesh: groups: 2 (over x), member: 8 (over z, y), tile: 2 (over core).
Axes of the slice: x: 2, y: 2, z: 4, core: 2. Of those that a mesh axis runs over, the one named last changes fastest.
Arguments:
- perturbations: bfloat16 [32, 3, 50, 16384], P(('groups', 'member'), None, None, 'tile'), parts along dimension 0, may hold values from -6 to 6
- control: float32 [32, 50, 16384], P(('groups', 'member'), None, 'tile'), parts along dimension 0, may hold values from -6 to 6
- loc_sqrt: float32 [50, 50], replicated, may hold values from 0 to 1
- gate_points: int32 [8, 32768], P(None, ('groups', 'member', 'tile')), parts along dimension 1, may hold values from 0 to 409599, as said below
- gate_weights: float32 [8, 32768], P(None, ('groups', 'member', 'tile')), parts along dimension 1, may hold values from 0.05 to 1
- gate_azimuth: float32 [32768], P(('groups', 'member', 'tile')), parts along dimension 0, may hold values from -3.140625 to 3.140625
- gate_elevation: float32 [32768], P(('groups', 'member', 'tile')), parts along dimension 0, may hold values from 0 to 0.5
- innovation: float32 [32768], P(('groups', 'member', 'tile')), parts along dimension 0, may hold values from -10 to 10
- obs_weight: float32 [32768], P(('groups', 'member', 'tile')), parts along dimension 0, may hold values from 0.25 to 4
- gate_counts: int32 [32], P(('groups', 'member', 'tile')), parts along dimension 0, may hold values from 256 to 1024, as said below
Outputs:
- gradient: float32 [32, 50, 16384], P(('groups', 'member'), None, 'tile'), parts along dimension 0
- gate_residual: float32 [32768], P(('groups', 'member', 'tile')), parts along dimension 0
There are 2 independent parts, one for each index of `groups`. A program takes and returns all parts, laid end to end along the dimension named above; an argument that names none is the same for every part. Nothing has to cross between parts.
Inputs may be any that keep to these rules, and one draw needn't show every extreme that they name: `gate_points`: column g lists the eight corners of one grid box of gate g's tile: with base level z, base x and base y, corner (a, b, c), c fastest, is (z + a) * 8192 + (x + b) * 128 + y + c. `gate_counts`: one block is full in every draw.
All inputs are finite; a program needn't handle non-finite values.
Results may differ from a plain program's by a relative error of at most 0.0003.
Values sent between devices are 32-bit elements; how exact they have to be, the bound alone decides.
A program may use at most 128 MiB of HBM per device.

v0:
```python
import functools

import jax
import jax.numpy as jnp
from jax import lax
from jax.experimental import pallas as pl
from jax.experimental.pallas import tpu as pltpu
from jax.sharding import PartitionSpec as P

LANES = 128
LEVEL_PAD = 56
DEPTH = 64
X_STEP = LEVEL_PAD * 3
CHUNK = 64
BUFFERS = 4
X_BLOCK = 8
MESH = pl.DeviceIdType.MESH
VMEM = 56 * 1024 * 1024


def split(value):
    high = value.astype(jnp.bfloat16)
    low = (value - high.astype(jnp.float32)).astype(jnp.bfloat16)
    return high, low


def level_product(matrix, value):
    m_high, m_low = split(matrix)
    v_high, v_low = split(value)
    left = jnp.concatenate([m_high, m_high, m_low], axis=1)
    right = jnp.concatenate([v_high, v_low, v_high], axis=0)
    return jnp.dot(left, right, preferred_element_type=jnp.float32)


def greet():
    axis, me = lax.axis_size("member"), lax.axis_index("member")
    barrier = pltpu.get_barrier_semaphore()
    for d in range(1, axis):
        pl.semaphore_signal(
            barrier, inc=1, device_id={"member": lax.rem(me + d, axis)}, device_id_type=MESH
        )
    pl.semaphore_wait(barrier, axis - 1)


def copies_out(source, slots_ref, send_sem, recv_sem):
    axis, me = lax.axis_size("member"), lax.axis_index("member")
    copies = []
    for d in range(1, axis):
        to = lax.rem(me + d, axis)
        copies.append(
            pltpu.make_async_remote_copy(
                src_ref=source(to),
                dst_ref=slots_ref.at[me],
                send_sem=send_sem.at[d - 1],
                recv_sem=recv_sem.at[d - 1],
                device_id={"member": to},
                device_id_type=MESH,
            )
        )
    return copies


def field_kernel(
    tile_cells, loc_ref, control_ref, pert_ref, points_ref, weights_ref, azimuth_ref,
    elevation_ref, innovation_ref, obs_ref, count_ref,
    field_ref, meta_ref, index_ref, counts_ref, side_ref,
    padded, pert_rows, own_ref, slots_ref, send_sem, recv_sem,
):
    axis, fields, slots = slots_ref.shape
    per = slots // LANES
    me = lax.axis_index("member")
    step = pl.program_id(0)

    @pl.when(step == 0)
    def _():
        padded[...] = jnp.zeros_like(padded)
        own_ref[0:8, :] = weights_ref[...]
        horizontal = jnp.cos(elevation_ref[...])
        own_ref[8:9, :] = horizontal * jnp.sin(azimuth_ref[...])
        own_ref[9:10, :] = horizontal * jnp.cos(azimuth_ref[...])
        own_ref[10:11, :] = jnp.sin(elevation_ref[...])
        own_ref[11:12, :] = innovation_ref[...]
        own_ref[12:13, :] = obs_ref[...]
        own_ref[13:14, :] = points_ref[0:1, :].astype(jnp.float32)
        own_ref[14:15, :] = jnp.full((1, slots), count_ref[0], jnp.int32).astype(jnp.float32)
        own_ref[15:16, :] = jnp.zeros((1, slots), jnp.float32)
        greet()
        for copy in copies_out(lambda to: own_ref, slots_ref, send_sem, recv_sem):
            copy.start()
        slots_ref[me] = own_ref[...]

    levels, across, lanes = control_ref.shape
    control_rows = control_ref.reshape(levels * across, lanes)
    for r in range(across):
        padded[0:levels, r * LANES : (r + 1) * LANES] = control_rows[
            pl.ds(r, levels, stride=across), :
        ]
    localized = level_product(loc_ref[...], padded[...])[0:levels]
    members = across // X_BLOCK
    for c in range(3):
        pert_rows[...] = pert_ref[c].astype(jnp.float32).reshape(levels * across, lanes)
        for x in range(X_BLOCK):
            total = None
            for k in range(members):
                r = x * members + k
                term = (
                    pert_rows[pl.ds(r, levels, stride=across), :]
                    * localized[:, r * LANES : (r + 1) * LANES]
                )
                total = term if k == 0 else total + term
            if c == 0:
                field_ref[x * X_STEP + 144 : (x + 1) * X_STEP, :] = jnp.zeros(
                    (X_STEP - 144, LANES), jnp.float32
                )
            field_ref[pl.ds(x * X_STEP + c, levels, stride=3), :] = total

    @pl.when(step == pl.num_programs(0) - 1)
    def _():
        for copy in copies_out(lambda to: own_ref, slots_ref, send_sem, recv_sem):
            copy.wait()
        slot = lax.broadcasted_iota(jnp.int32, (1, slots), 1)
        for d in range(axis):
            meta_ref[d] = slots_ref[d]
            base = slots_ref[d, 13:14, :].astype(jnp.int32)
            count = slots_ref[d, 14:15, :].astype(jnp.int32)
            level = lax.div(base, jnp.int32(tile_cells))
            inside = base - level * tile_cells
            column = lax.div(inside, jnp.int32(LANES))
            position = inside - column * LANES
            index = (column * LEVEL_PAD + level) * (3 * LANES) + ((slot - position) & (LANES - 1))
            live = jnp.where(slot < count, 1.0, 0.0)
            innovation = slots_ref[d, 11:12, :]
            weight = slots_ref[d, 12:13, :]
            counts_ref[d : d + 1, :] = count[:, 0:LANES]
            for q in range(per):
                row = d * per + q
                at = slice(q * LANES, (q + 1) * LANES)
                index_ref[row : row + 1, :] = index[:, at]
                side_ref[0, row : row + 1, :] = live[:, at]
                side_ref[1, row : row + 1, :] = innovation[:, at]
                side_ref[2, row : row + 1, :] = weight[:, at]


def residual_kernel(
    factor, partial_ref, side_ref, weighted_ref, residual_ref,
    parts_ref, done_ref, send_sem, recv_sem, send_done, recv_done,
):
    axis, per, lanes = parts_ref.shape
    me = lax.axis_index("member")
    greet()
    sums = copies_out(
        lambda to: partial_ref.at[pl.ds(pl.multiple_of(to * per, per), per), :],
        parts_ref, send_sem, recv_sem,
    )
    for copy in sums:
        copy.start()
    own = pl.ds(pl.multiple_of(me * per, per), per)
    parts_ref[me] = partial_ref[own, :]
    for copy in sums:
        copy.wait()
    total = parts_ref[0]
    for d in range(1, axis):
        total = total + parts_ref[d]
    residual = side_ref[0, own, :] * (factor * total - side_ref[1, own, :])
    residual_ref[...] = residual
    done_ref[me] = side_ref[2, own, :] * residual
    results = copies_out(lambda to: done_ref.at[me], done_ref, send_done, recv_done)
    for copy in results:
        copy.start()
    for copy in results:
        copy.wait()
    for d in range(axis):
        weighted_ref[d * per : (d + 1) * per, :] = done_ref[d]


def gate_factors(meta_ref, block, lanes):
    weight = meta_ref[block, 0:8, lanes]
    coeff = meta_ref[block, 8:16, lanes]
    row = lax.broadcasted_iota(jnp.int32, (8, LANES), 0)
    component = row % 3
    by_row = jnp.where(
        component == 0, coeff[0:1], jnp.where(component == 1, coeff[1:2], coeff[2:3])
    )
    factors = {}
    for b in range(2):
        for c in range(2):
            p = 2 * b + c
            corner = jnp.where(
                row < 3, weight[p : p + 1], jnp.where(row < 6, weight[4 + p : 5 + p], 0.0)
            )
            factors[b, c] = corner * by_row
    return factors


def over_groups(counts_ref, slots, visit):
    def block_body(block, carry):
        count = counts_ref[block * LANES]

        def group_body(group, inner):
            left = jnp.minimum(count - group * LANES, LANES)
            visit(block, group, (left + CHUNK - 1) // CHUNK)
            return inner

        lax.fori_loop(0, (count + LANES - 1) // LANES, group_body, 0)
        return carry

    lax.fori_loop(0, counts_ref.shape[0] // LANES, block_body, 0)


def gather_kernel(counts_ref, index_ref, meta_ref, field_ref, out_ref):
    slots = meta_ref.shape[2]
    groups = slots // LANES
    out_ref[...] = jnp.zeros_like(out_ref)
    lane = lax.broadcasted_iota(jnp.int32, (8, LANES), 1)

    def visit(block, group, chunks):
        first = block * slots + group * LANES

        def chunk_body(chunk, acc):
            a00, a01, a10, a11 = acc
            slot = chunk * CHUNK
            shifted = lane - slot
            here = shifted == 0
            for i in range(CHUNK):
                packed = index_ref[first + slot + i]
                row = packed >> 7
                shift = packed & 127
                near = pltpu.roll(field_ref[pl.ds(row, 8), :], shift, axis=1)
                far = pltpu.roll(field_ref[pl.ds(row + X_STEP, 8), :], shift, axis=1)
                if i < CHUNK - 1:
                    after = shifted == i + 1
                else:
                    after = lane == ((slot + CHUNK) & 127)
                a00 = jnp.where(here, near, a00)
                a01 = jnp.where(after, near, a01)
                a10 = jnp.where(here, far, a10)
                a11 = jnp.where(after, far, a11)
                here = after
            return a00, a01, a10, a11

        zero = jnp.zeros((8, LANES), jnp.float32)
        a00, a01, a10, a11 = lax.fori_loop(0, chunks, chunk_body, (zero, zero, zero, zero))
        factors = gate_factors(meta_ref, block, pl.ds(pl.multiple_of(group * LANES, LANES), LANES))
        value = (
            a00 * factors[0, 0]
            + pltpu.roll(a01, LANES - 1, axis=1) * factors[0, 1]
            + a10 * factors[1, 0]
            + pltpu.roll(a11, LANES - 1, axis=1) * factors[1, 1]
        )
        out_ref[pl.ds(block * groups + group, 1), :] = jnp.sum(value, axis=0, keepdims=True)

    over_groups(counts_ref, slots, visit)


def scatter_kernel(
    factor, counts_ref, index_ref, meta_ref, weighted_ref, loc_ref, control_ref, pert_ref,
    out_ref, buffers, padded, pert_rows,
):
    levels, across, lanes = control_ref.shape
    slots = meta_ref.shape[2]
    groups = slots // LANES
    step = pl.program_id(0)

    @pl.when(step == 0)
    def _():
        padded[...] = jnp.zeros_like(padded)
        rows = buffers.shape[1]
        per = X_STEP

        def clear(i, carry):
            at = pl.ds(pl.multiple_of(i * per, per), per)
            for j in range(BUFFERS):
                buffers[j, at, :] = jnp.zeros((per, LANES), jnp.float32)
            return carry

        lax.fori_loop(0, rows // per, clear, 0)
        lane = lax.broadcasted_iota(jnp.int32, (8, LANES), 1)

        def visit(block, group, chunks):
            first = block * slots + group * LANES
            factors = gate_factors(
                meta_ref, block, pl.ds(pl.multiple_of(group * LANES, LANES), LANES)
            )
            amount = weighted_ref[pl.ds(block * groups + group, 1), :]
            a00 = factors[0, 0] * amount
            a01 = pltpu.roll(factors[0, 1] * amount, 1, axis=1)
            a10 = factors[1, 0] * amount
            a11 = pltpu.roll(factors[1, 1] * amount, 1, axis=1)

            def chunk_body(chunk, carry):
                slot = chunk * CHUNK
                shifted = lane - slot
                here = shifted == 0
                for i0 in range(0, CHUNK, BUFFERS):
                    added = []
                    for j in range(BUFFERS):
                        i = i0 + j
                        packed = index_ref[first + slot + i]
                        row = packed >> 7
                        shift = (-packed) & 127
                        if i < CHUNK - 1:
                            after = shifted == i + 1
                        else:
                            after = lane == ((slot + CHUNK) & 127)
                        near = jnp.where(here, a00, jnp.where(after, a01, 0.0))
                        far = jnp.where(here, a10, jnp.where(after, a11, 0.0))
                        here = after
                        added.append(
                            (
                                pl.ds(row, 8),
                                pl.ds(row + X_STEP, 8),
                                pltpu.roll(near, shift, axis=1),
                                pltpu.roll(far, shift, axis=1),
                            )
                        )
                    held = [
                        (buffers[j, added[j][0], :], buffers[j, added[j][1], :])
                        for j in range(BUFFERS)
                    ]
                    for j in range(BUFFERS):
                        buffers[j, added[j][0], :] = held[j][0] + added[j][2]
                        buffers[j, added[j][1], :] = held[j][1] + added[j][3]
                return carry

            lax.fori_loop(0, chunks, chunk_body, 0)

        over_groups(counts_ref, slots, visit)

    members = across // X_BLOCK
    for c in range(3):
        pert_rows[...] = pert_ref[c].astype(jnp.float32).reshape(levels * across, lanes)
        for x in range(X_BLOCK):
            at = pl.ds((step * X_BLOCK + x) * X_STEP + c, levels, stride=3)
            adjoint = buffers[0, at, :]
            for j in range(1, BUFFERS):
                adjoint = adjoint + buffers[j, at, :]
            for k in range(members):
                r = x * members + k
                here = slice(r * LANES, (r + 1) * LANES)
                term = pert_rows[pl.ds(r, levels, stride=across), :] * adjoint
                if c == 0:
                    padded[0:levels, here] = term
                else:
                    padded[0:levels, here] = padded[0:levels, here] + term
    product = level_product(loc_ref[...], padded[...])
    control_rows = control_ref.reshape(levels * across, lanes)
    out_rows = out_ref.reshape(levels * across, lanes)
    for r in range(across):
        at = pl.ds(r, levels, stride=across)
        out_rows[at, :] = (
            control_rows[at, :] + factor * product[0:levels, r * LANES : (r + 1) * LANES]
        )


def whole(shape):
    return pl.BlockSpec(shape, lambda *i: (0,) * len(shape))


def local(
    perturbations,
    control,
    loc_sqrt,
    gate_points,
    gate_weights,
    gate_azimuth,
    gate_elevation,
    innovation,
    obs_weight,
    gate_counts,
):
    mem_dev, components, levels, tile_cells = perturbations.shape
    slots = gate_points.shape[1]
    axis = lax.axis_size("member")
    factor = (mem_dev * axis - 1) ** (-0.5)
    columns = tile_cells // LANES
    rows = columns * X_STEP
    groups = axis * slots // LANES
    vmem = pl.BlockSpec(memory_space=pltpu.VMEM)
    smem = pl.BlockSpec(memory_space=pltpu.SMEM)
    semaphores = [pltpu.SemaphoreType.DMA((axis - 1,)), pltpu.SemaphoreType.DMA((axis - 1,))]
    across = X_BLOCK * mem_dev
    control_view = (
        control.reshape(mem_dev, levels, columns, LANES)
        .transpose(1, 2, 0, 3)
        .reshape(levels, columns * mem_dev, LANES)
    )
    pert_view = (
        perturbations.reshape(mem_dev, 3, levels, columns, LANES)
        .transpose(1, 2, 3, 0, 4)
        .reshape(3, levels, columns * mem_dev, LANES)
    )
    loc_pad = jnp.pad(loc_sqrt, ((0, DEPTH - levels), (0, DEPTH - levels)))
    pert_spec = pl.BlockSpec((3, levels, across, LANES), lambda i: (0, 0, i, 0))
    control_spec = pl.BlockSpec((levels, across, LANES), lambda i: (0, i, 0))
    dense = [
        pltpu.VMEM((DEPTH, across * LANES), jnp.float32),
        pltpu.VMEM((levels * across, LANES), jnp.float32),
    ]
    row = whole((1, slots))
    field, meta, index, counts, side = pl.pallas_call(
        functools.partial(field_kernel, tile_cells),
        grid=(columns // X_BLOCK,),
        out_shape=(
            jax.ShapeDtypeStruct((rows, LANES), jnp.float32),
            jax.ShapeDtypeStruct((axis, 16, slots), jnp.float32),
            jax.ShapeDtypeStruct((groups, LANES), jnp.int32),
            jax.ShapeDtypeStruct((axis, LANES), jnp.int32),
            jax.ShapeDtypeStruct((3, groups, LANES), jnp.float32),
        ),
        in_specs=[
            whole((DEPTH, DEPTH)),
            control_spec,
            pert_spec,
            whole((8, slots)),
            whole((8, slots)),
            row,
            row,
            row,
            row,
            smem,
        ],
        out_specs=(
            pl.BlockSpec((X_BLOCK * X_STEP, LANES), lambda i: (i, 0)),
            whole((axis, 16, slots)),
            whole((groups, LANES)),
            whole((axis, LANES)),
            whole((3, groups, LANES)),
        ),
        scratch_shapes=[
            *dense,
            pltpu.VMEM((16, slots), jnp.float32),
            pltpu.VMEM((axis, 16, slots), jnp.float32),
            *semaphores,
        ],
        compiler_params=pltpu.CompilerParams(
            collective_id=0, has_side_effects=True, vmem_limit_bytes=VMEM
        ),
        name="field",
    )(
        loc_pad,
        control_view,
        pert_view,
        gate_points,
        gate_weights,
        gate_azimuth.reshape(1, slots),
        gate_elevation.reshape(1, slots),
        innovation.reshape(1, slots),
        obs_weight.reshape(1, slots),
        gate_counts,
    )
    index, counts = index.reshape(-1), counts.reshape(-1)

    partial = pl.pallas_call(
        gather_kernel,
        out_shape=jax.ShapeDtypeStruct((groups, LANES), jnp.float32),
        in_specs=[smem, smem, vmem, vmem],
        out_specs=vmem,
        compiler_params=pltpu.CompilerParams(vmem_limit_bytes=VMEM),
        name="gather",
    )(counts, index, meta, field)

    weighted, residual = pl.pallas_call(
        functools.partial(residual_kernel, factor),
        out_shape=(
            jax.ShapeDtypeStruct((groups, LANES), jnp.float32),
            jax.ShapeDtypeStruct((slots // LANES, LANES), jnp.float32),
        ),
        in_specs=[vmem, vmem],
        out_specs=(vmem, vmem),
        scratch_shapes=[
            pltpu.VMEM((axis, slots // LANES, LANES), jnp.float32),
            pltpu.VMEM((axis, slots // LANES, LANES), jnp.float32),
            *semaphores,
            *semaphores,
        ],
        compiler_params=pltpu.CompilerParams(
            collective_id=1, has_side_effects=True, vmem_limit_bytes=VMEM
        ),
        name="residual",
    )(partial, side)
    gate_residual = residual.reshape(slots)

    gradient = pl.pallas_call(
        functools.partial(scatter_kernel, factor),
        grid=(columns // X_BLOCK,),
        out_shape=jax.ShapeDtypeStruct((levels, columns * mem_dev, LANES), jnp.float32),
        in_specs=[
            smem,
            smem,
            whole(meta.shape),
            whole((groups, LANES)),
            whole((DEPTH, DEPTH)),
            control_spec,
            pert_spec,
        ],
        out_specs=control_spec,
        scratch_shapes=[
            pltpu.VMEM((BUFFERS, rows, LANES), jnp.float32),
            *dense,
        ],
        compiler_params=pltpu.CompilerParams(vmem_limit_bytes=VMEM),
        name="scatter",
    )(counts, index, meta, weighted, loc_pad.T, control_view, pert_view)
    gradient = (
        gradient.reshape(levels, columns, mem_dev, LANES)
        .transpose(2, 0, 1, 3)
        .reshape(mem_dev, levels, tile_cells)
    )
    return (gradient, gate_residual)


def solution(mesh):
    by_gate = P(("groups", "member", "tile"))
    return jax.shard_map(
        local,
        mesh=mesh,
        in_specs=(
            P(("groups", "member"), None, None, "tile"),
            P(("groups", "member"), None, "tile"),
            P(),
            P(None, ("groups", "member", "tile")),
            P(None, ("groups", "member", "tile")),
            by_gate,
            by_gate,
            by_gate,
            by_gate,
            by_gate,
        ),
        out_specs=(P(("groups", "member"), None, "tile"), by_gate),
        check_vma=False,
    )
```

profile of v0, /device:TPU:0, one launch (start us, length us, event | category | flops | bytes accessed | tf_op | source)
XLA Modules:
  0.0 108.7 jit_solution(12232120657347139803)
XLA Ops:
  0.6 0.8 copy.12
  1.5 0.1 copy.17
  1.6 0.6 pad.4.clone.loc_ref
  2.8 17.4 %field.1 = (f32[10752,128]{1,0:T(8,128)}, f32[8,16,1024]{2,1,0:T(8,128)}, s32[64,128]{1,0:T(8,128)}, s32[8,128]{1,0:T(8,128)}, f32[3,64,128]{2,1,0:T(8,128)}) custom-call(f32[64,64]{1,0:T(8,128)} %pad.4.clone.loc_ref, f32[50,128,128]{2,1,0:T(8,128)} %bitcast.26, bf16[3,50,128,128]{3,2,1,0:T(8,128)(2,1)} %bitcast.24, s32[8,1024]{1,0:T(8,128)} %points_ref.1, ...), custom_call_target="tpu_custom_call" | custom-call | tf_op jit(solution)/shard_map/field/pallas_call | solution.py:400
  20.2 29.0 %gather.1.partial_ref = f32[64,128]{1,0:T(8,128)} custom-call(s32[1024]{0:T(1024)} %bitcast.31, s32[8192]{0:T(1024)} %bitcast.29, f32[8,16,1024]{2,1,0:T(8,128)} %get-tuple-element.11.meta_ref, f32[10752,128]{1,0:T(8,128)} %get-tuple-element.12.field_ref), custom_call_target="tpu_custom_call" | custom-call | tf_op jit(solution)/shard_map/gather/pallas_call | solution.py:453
  49.3 16.8 %residual.1 = (f32[64,128]{1,0:T(8,128)}, f32[8,128]{1,0:T(8,128)}) custom-call(f32[64,128]{1,0:T(8,128)} %gather.1.partial_ref, f32[3,64,128]{2,1,0:T(8,128)} %get-tuple-element.13.side_ref), custom_call_target="tpu_custom_call" | custom-call | tf_op jit(solution)/shard_map/residual/pallas_call | solution.py:462
  66.1 0.6 pad_bitcast_fusion.loc_ref
  66.7 0.0 copy-start
  66.7 41.4 %scatter.1 = f32[50,128,128]{2,1,0:T(8,128)} custom-call(s32[1024]{0:T(1024)} %bitcast.32, s32[8192]{0:T(1024)} %bitcast.30, f32[8,16,1024]{2,1,0:T(8,128)} %get-tuple-element.11.meta_ref, f32[64,128]{1,0:T(8,128)} %get-tuple-element.14.weighted_ref, f32[64,64]{1,0:T(8,128)} %pad_bitcast_fusion.loc_ref, f32[50,128,128]{2,1,0:T(8,128)} %bitcast.27, ...), custom_call_target="tpu_custom_call" | custom-call | tf_op jit(solution)/shard_map/scatter/pallas_call | solution.py:483
  108.1 0.0 copy-done
  108.1 0.6 copy.20
Async XLA Ops:
  66.7 41.4 %copy-start = (f32[8,128]{1,0:T(8,128)S(1)}, f32[8,128]{1,0:T(8,128)}, u32[]{:S(2)}) copy-start(f32[8,128]{1,0:T(8,128)} %get-tuple-element.15) | copy-start | bytes 12292
where the time goes:
time: 109 us
  Pallas kernels  105 us (96%)
  local copies, waits for them, and re-layouts  2.79 us (3%)
  between operations  1.3 us (1%)
    pallas_call x1, Pallas kernels, local(): pl.pallas_call(functools.partial(scatter_kernel, factor), grid=(columns /...  41.4 us
    pallas_call x1, Pallas kernels, local(): pl.pallas_call(gather_kernel, out_shape=jax.ShapeDtypeStruct((groups, LAN...  29 us
    pallas_call x1, Pallas kernels, local(): pl.pallas_call(functools.partial(field_kernel, tile_cells), grid=(columns...  17.4 us
    pallas_call x1, Pallas kernels, local(): pl.pallas_call(functools.partial(residual_kernel, factor), out_shape=(jax...  16.8 us

commit v1 on v0

--- a/solution.py
+++ b/solution.py
@@ -11,9 +11,10 @@
 LEVEL_PAD = 56
 DEPTH = 64
 X_STEP = LEVEL_PAD * 3
-CHUNK = 64
+CHUNK = 128
 BUFFERS = 4
 X_BLOCK = 8
+FORWARD_STEP = 4
 MESH = pl.DeviceIdType.MESH
 VMEM = 56 * 1024 * 1024
 
@@ -24,12 +25,21 @@
     return high, low
 
 
-def level_product(matrix, value):
+def level_product(matrix, value, flipped):
     m_high, m_low = split(matrix)
     v_high, v_low = split(value)
-    left = jnp.concatenate([m_high, m_high, m_low], axis=1)
+    side = 0 if flipped else 1
+    left = jnp.concatenate([m_high, m_high, m_low], axis=side)
     right = jnp.concatenate([v_high, v_low, v_high], axis=0)
-    return jnp.dot(left, right, preferred_element_type=jnp.float32)
+    return lax.dot_general(
+        left, right, (((side,), (0,)), ((), ())), preferred_element_type=jnp.float32
+    )
+
+
+def pad_matrix(loc_ref, loc_pad):
+    levels = loc_ref.shape[0]
+    loc_pad[...] = jnp.zeros_like(loc_pad)
+    loc_pad[0:levels, 0:levels] = loc_ref[...]
 
 
 def greet():
@@ -60,11 +70,37 @@
     return copies
 
 
+def block_copies(own_ref, slots_ref, send_sem, recv_sem):
+    axis, me = lax.axis_size("member"), lax.axis_index("member")
+    partner = me + 1 - 2 * lax.rem(me, 2)
+
+    def send(source, slot, order, to):
+        return pltpu.make_async_remote_copy(
+            src_ref=source,
+            dst_ref=slots_ref.at[slot],
+            send_sem=send_sem.at[order],
+            recv_sem=recv_sem.at[order],
+            device_id={"member": to},
+            device_id_type=MESH,
+        )
+
+    half = axis // 2
+    first = [
+        send(own_ref, me, d - 1, lax.rem(me + 2 * d, axis)) for d in range(1, half)
+    ]
+    across = send(own_ref, me, half - 1, partner)
+    passed = []
+    for d in range(1, half):
+        came = lax.rem(me - 2 * d + axis, axis)
+        passed.append(send(slots_ref.at[came], came, half + d - 1, partner))
+    return first, across, passed
+
+
 def field_kernel(
     tile_cells, loc_ref, control_ref, pert_ref, points_ref, weights_ref, azimuth_ref,
     elevation_ref, innovation_ref, obs_ref, count_ref,
     field_ref, meta_ref, index_ref, counts_ref, side_ref,
-    padded, pert_rows, own_ref, slots_ref, send_sem, recv_sem,
+    padded, pert_rows, loc_pad, own_ref, slots_ref, send_sem, recv_sem,
 ):
     axis, fields, slots = slots_ref.shape
     per = slots // LANES
@@ -74,6 +110,7 @@
     @pl.when(step == 0)
     def _():
         padded[...] = jnp.zeros_like(padded)
+        pad_matrix(loc_ref, loc_pad)
         own_ref[0:8, :] = weights_ref[...]
         horizontal = jnp.cos(elevation_ref[...])
         own_ref[8:9, :] = horizontal * jnp.sin(azimuth_ref[...])
@@ -85,8 +122,10 @@
         own_ref[14:15, :] = jnp.full((1, slots), count_ref[0], jnp.int32).astype(jnp.float32)
         own_ref[15:16, :] = jnp.zeros((1, slots), jnp.float32)
         greet()
-        for copy in copies_out(lambda to: own_ref, slots_ref, send_sem, recv_sem):
+        first, across_copy, passed = block_copies(own_ref, slots_ref, send_sem, recv_sem)
+        for copy in first:
             copy.start()
+        across_copy.start()
         slots_ref[me] = own_ref[...]
 
     levels, across, lanes = control_ref.shape
@@ -95,7 +134,7 @@
         padded[0:levels, r * LANES : (r + 1) * LANES] = control_rows[
             pl.ds(r, levels, stride=across), :
         ]
-    localized = level_product(loc_ref[...], padded[...])[0:levels]
+    localized = level_product(loc_pad[...], padded[...], False)[0:levels]
     members = across // X_BLOCK
     for c in range(3):
         pert_rows[...] = pert_ref[c].astype(jnp.float32).reshape(levels * across, lanes)
@@ -114,9 +153,20 @@
                 )
             field_ref[pl.ds(x * X_STEP + c, levels, stride=3), :] = total
 
+    @pl.when(step == FORWARD_STEP)
+    def _():
+        first, across_copy, passed = block_copies(own_ref, slots_ref, send_sem, recv_sem)
+        for came, on in zip(first, passed):
+            came.wait_recv()
+            on.start()
+
     @pl.when(step == pl.num_programs(0) - 1)
     def _():
-        for copy in copies_out(lambda to: own_ref, slots_ref, send_sem, recv_sem):
+        first, across_copy, passed = block_copies(own_ref, slots_ref, send_sem, recv_sem)
+        for copy in first:
+            copy.wait_send()
+        across_copy.wait()
+        for copy in passed:
             copy.wait()
         slot = lax.broadcasted_iota(jnp.int32, (1, slots), 1)
         for d in range(axis):
@@ -254,7 +304,7 @@
 
 def scatter_kernel(
     factor, counts_ref, index_ref, meta_ref, weighted_ref, loc_ref, control_ref, pert_ref,
-    out_ref, buffers, padded, pert_rows,
+    out_ref, buffers, padded, pert_rows, loc_pad,
 ):
     levels, across, lanes = control_ref.shape
     slots = meta_ref.shape[2]
@@ -264,6 +314,7 @@
     @pl.when(step == 0)
     def _():
         padded[...] = jnp.zeros_like(padded)
+        pad_matrix(loc_ref, loc_pad)
         rows = buffers.shape[1]
         per = X_STEP
 
@@ -342,7 +393,7 @@
                     padded[0:levels, here] = term
                 else:
                     padded[0:levels, here] = padded[0:levels, here] + term
-    product = level_product(loc_ref[...], padded[...])
+    product = level_product(loc_pad[...], padded[...], True)
     control_rows = control_ref.reshape(levels * across, lanes)
     out_rows = out_ref.reshape(levels * across, lanes)
     for r in range(across):
@@ -389,12 +440,12 @@
         .transpose(1, 2, 3, 0, 4)
         .reshape(3, levels, columns * mem_dev, LANES)
     )
-    loc_pad = jnp.pad(loc_sqrt, ((0, DEPTH - levels), (0, DEPTH - levels)))
     pert_spec = pl.BlockSpec((3, levels, across, LANES), lambda i: (0, 0, i, 0))
     control_spec = pl.BlockSpec((levels, across, LANES), lambda i: (0, i, 0))
     dense = [
         pltpu.VMEM((DEPTH, across * LANES), jnp.float32),
         pltpu.VMEM((levels * across, LANES), jnp.float32),
+        pltpu.VMEM((DEPTH, DEPTH), jnp.float32),
     ]
     row = whole((1, slots))
     field, meta, index, counts, side = pl.pallas_call(
@@ -408,7 +459,7 @@
             jax.ShapeDtypeStruct((3, groups, LANES), jnp.float32),
         ),
         in_specs=[
-            whole((DEPTH, DEPTH)),
+            whole((levels, levels)),
             control_spec,
             pert_spec,
             whole((8, slots)),
@@ -437,7 +488,7 @@
         ),
         name="field",
     )(
-        loc_pad,
+        loc_sqrt,
         control_view,
         pert_view,
         gate_points,
@@ -489,7 +540,7 @@
             smem,
             whole(meta.shape),
             whole((groups, LANES)),
-            whole((DEPTH, DEPTH)),
+            whole((levels, levels)),
             control_spec,
             pert_spec,
         ],
@@ -500,7 +551,7 @@
         ],
         compiler_params=pltpu.CompilerParams(vmem_limit_bytes=VMEM),
         name="scatter",
-    )(counts, index, meta, weighted, loc_pad.T, control_view, pert_view)
+    )(counts, index, meta, weighted, loc_sqrt, control_view, pert_view)
     gradient = (
         gradient.reshape(levels, columns, mem_dev, LANES)
         .transpose(2, 0, 1, 3)

time: 109 us -> 95.6 us (0.88)
  the two profiles are of different devices: /device:TPU:0 before, /device:TPU:2 now
where the time goes in v1:
time: 95.6 us; the launch traced here: 96.6 us
  Pallas kernels  94.7 us (99%)
  between operations  1.3 us (1%)
    pallas_call x1, Pallas kernels, local(): pl.pallas_call(functools.partial(scatter_kernel, factor), grid=(columns /...  38.1 us
    pallas_call x1, Pallas kernels, local(): pl.pallas_call(gather_kernel, out_shape=jax.ShapeDtypeStruct((groups, LAN...  26 us
    pallas_call x1, Pallas kernels, local(): pl.pallas_call(functools.partial(field_kernel, tile_cells), grid=(columns...  17.9 us
    pallas_call x1, Pallas kernels, local(): pl.pallas_call(functools.partial(residual_kernel, factor), out_shape=(jax...  12.8 us

profile of v1, /device:TPU:2, one launch (start us, length us, event | category | flops | bytes accessed | tf_op | source)
XLA Modules:
  0.0 96.6 jit_solution(17514241169416120065)
XLA Ops:
  1.3 17.9 %field.1 = (f32[10752,128]{1,0:T(8,128)}, f32[8,16,1024]{2,1,0:T(8,128)}, s32[64,128]{1,0:T(8,128)}, s32[8,128]{1,0:T(8,128)}, f32[3,64,128]{2,1,0:T(8,128)}) custom-call(f32[50,50]{1,0:T(8,128)} %loc_ref.3, f32[50,128,128]{2,1,0:T(8,128)} %bitcast.24, bf16[3,50,128,128]{3,2,1,0:T(8,128)(2,1)} %bitcast.22, s32[8,1024]{1,0:T(8,128)} %points_ref.1, ...), custom_call_target="tpu_custom_call" | custom-call | tf_op jit(solution)/shard_map/field/pallas_call | solution.py:451
  19.2 26.0 %gather.1.partial_ref = f32[64,128]{1,0:T(8,128)} custom-call(s32[1024]{0:T(1024)} %bitcast.29, s32[8192]{0:T(1024)} %bitcast.27, f32[8,16,1024]{2,1,0:T(8,128)} %get-tuple-element.11.meta_ref, f32[10752,128]{1,0:T(8,128)} %get-tuple-element.12.field_ref), custom_call_target="tpu_custom_call" | custom-call | tf_op jit(solution)/shard_map/gather/pallas_call | solution.py:504
  45.1 12.8 %residual.1 = (f32[64,128]{1,0:T(8,128)}, f32[8,128]{1,0:T(8,128)}) custom-call(f32[64,128]{1,0:T(8,128)} %gather.1.partial_ref, f32[3,64,128]{2,1,0:T(8,128)} %get-tuple-element.13.side_ref), custom_call_target="tpu_custom_call" | custom-call | tf_op jit(solution)/shard_map/residual/pallas_call | solution.py:513
  57.9 0.0 copy-start
  57.9 38.1 %scatter.1 = f32[50,128,128]{2,1,0:T(8,128)} custom-call(s32[1024]{0:T(1024)} %bitcast.30, s32[8192]{0:T(1024)} %bitcast.28, f32[8,16,1024]{2,1,0:T(8,128)} %get-tuple-element.11.meta_ref, f32[64,128]{1,0:T(8,128)} %get-tuple-element.14.weighted_ref, f32[50,50]{1,0:T(8,128)} %loc_ref.3, f32[50,128,128]{2,1,0:T(8,128)} %bitcast.25, ...), custom_call_target="tpu_custom_call" | custom-call | tf_op jit(solution)/shard_map/scatter/pallas_call | solution.py:534
  96.0 0.0 copy-done
  96.0 0.6 copy.17
Async XLA Ops:
  57.9 38.1 %copy-start = (f32[8,128]{1,0:T(8,128)S(1)}, f32[8,128]{1,0:T(8,128)}, u32[]{:S(2)}) copy-start(f32[8,128]{1,0:T(8,128)} %get-tuple-element.15) | copy-start | bytes 12292

commit v2 on v1

--- a/solution.py
+++ b/solution.py
@@ -13,8 +13,8 @@
 X_STEP = LEVEL_PAD * 3
 CHUNK = 128
 BUFFERS = 4
-X_BLOCK = 8
-FORWARD_STEP = 4
+X_BLOCK = 16
+FORWARD_STEP = 2
 MESH = pl.DeviceIdType.MESH
 VMEM = 56 * 1024 * 1024
 

time: 95.6 us -> 98.3 us (1.028)
  the two profiles are of different devices: /device:TPU:2 before, /device:TPU:0 now
where the time goes in v2:
time: 98.3 us; the launch traced here: 96.8 us
  Pallas kernels  94.9 us (97%)
  between operations  1.3 us (1%)
    pallas_call x1, Pallas kernels, local(): pl.pallas_call(functools.partial(scatter_kernel, factor), grid=(columns /...  39.1 us
    pallas_call x1, Pallas kernels, local(): pl.pallas_call(functools.partial(field_kernel, tile_cells), grid=(columns...  23 us
    pallas_call x1, Pallas kernels, local(): pl.pallas_call(gather_kernel, out_shape=jax.ShapeDtypeStruct((groups, LAN...  21.3 us
    pallas_call x1, Pallas kernels, local(): pl.pallas_call(functools.partial(residual_kernel, factor), out_shape=(jax...  11.5 us

profile of v2, /device:TPU:0, one launch (start us, length us, event | category | flops | bytes accessed | tf_op | source)
XLA Modules:
  0.0 96.8 jit_solution(15531695741581984413)
XLA Ops:
  1.3 23.0 %field.1 = (f32[10752,128]{1,0:T(8,128)}, f32[8,16,1024]{2,1,0:T(8,128)}, s32[64,128]{1,0:T(8,128)}, s32[8,128]{1,0:T(8,128)}, f32[3,64,128]{2,1,0:T(8,128)}) custom-call(f32[50,50]{1,0:T(8,128)} %loc_ref.3, f32[50,128,128]{2,1,0:T(8,128)} %bitcast.24, bf16[3,50,128,128]{3,2,1,0:T(8,128)(2,1)} %bitcast.22, s32[8,1024]{1,0:T(8,128)} %points_ref.1, ...), custom_call_target="tpu_custom_call" | custom-call | tf_op jit(solution)/shard_map/field/pallas_call | solution.py:451
  24.3 21.3 %gather.1.partial_ref = f32[64,128]{1,0:T(8,128)} custom-call(s32[1024]{0:T(1024)} %bitcast.29, s32[8192]{0:T(1024)} %bitcast.27, f32[8,16,1024]{2,1,0:T(8,128)} %get-tuple-element.11.meta_ref, f32[10752,128]{1,0:T(8,128)} %get-tuple-element.12.field_ref), custom_call_target="tpu_custom_call" | custom-call | tf_op jit(solution)/shard_map/gather/pallas_call | solution.py:504
  45.5 11.5 %residual.1 = (f32[64,128]{1,0:T(8,128)}, f32[8,128]{1,0:T(8,128)}) custom-call(f32[64,128]{1,0:T(8,128)} %gather.1.partial_ref, f32[3,64,128]{2,1,0:T(8,128)} %get-tuple-element.13.side_ref), custom_call_target="tpu_custom_call" | custom-call | tf_op jit(solution)/shard_map/residual/pallas_call | solution.py:513
  57.1 0.0 copy-start
  57.1 39.1 %scatter.1 = f32[50,128,128]{2,1,0:T(8,128)} custom-call(s32[1024]{0:T(1024)} %bitcast.30, s32[8192]{0:T(1024)} %bitcast.28, f32[8,16,1024]{2,1,0:T(8,128)} %get-tuple-element.11.meta_ref, f32[64,128]{1,0:T(8,128)} %get-tuple-element.14.weighted_ref, f32[50,50]{1,0:T(8,128)} %loc_ref.3, f32[50,128,128]{2,1,0:T(8,128)} %bitcast.25, ...), custom_call_target="tpu_custom_call" | custom-call | tf_op jit(solution)/shard_map/scatter/pallas_call | solution.py:534
  96.2 0.0 copy-done
  96.2 0.6 copy.17
Async XLA Ops:
  57.1 39.1 %copy-start = (f32[8,128]{1,0:T(8,128)S(1)}, f32[8,128]{1,0:T(8,128)}, u32[]{:S(2)}) copy-start(f32[8,128]{1,0:T(8,128)} %get-tuple-element.15) | copy-start | bytes 12292
